TPU v7x, 32 devices: a whole 2x2x4 slice. The times are simulated.
32 devices in a mesh: row: 16 (over z, y, x), ps: 2 (over core).
Axes of the slice: x: 2, y: 2, z: 4, core: 2. Of those that a mesh axis runs over, the one named last changes fastest.
Arguments:
- flow_state: float32 [128, 5, 16, 4, 128], P('row', None, None, 'ps'), may hold values from -1.6 to 1.6
- forcing: float32 [128, 5, 16, 4, 128], P('row', None, None, 'ps'), may hold values from -1.6 to 1.6
- harmonic_op: float32 [16, 16], replicated, may hold values from -1.5 to 1.5
- diag_inv: float32 [128, 5, 5, 4, 128], P('row', None, None, 'ps'), may hold values from -0.02 to 0.275
- lower_coupling: float32 [128, 5, 5, 4, 128], P('row', None, None, 'ps'), may hold values from -4.81 to 0.36
- upper_coupling: float32 [128, 5, 5, 4, 128], P('row', None, None, 'ps'), may hold values from -4.81 to 0.36
Outputs:
- residual: float32 [128, 5, 16, 4, 128], P('row', None, None, 'ps')
- correction: float32 [128, 5, 16, 4, 128], P('row', None, None, 'ps')
All inputs are finite; a program needn't handle non-finite values.
Results may differ from a plain program's by a relative error of at most 0.00016.
Values sent between devices are 32-bit elements; how exact they have to be, the bound alone decides.
A program may use at most 192 MiB of HBM per device.

v0:
```python
import functools

import jax
import jax.numpy as jnp
from jax import lax
from jax.experimental import pallas as pl
from jax.experimental.pallas import tpu as pltpu
from jax.sharding import PartitionSpec as P

MESH = pl.DeviceIdType.MESH
HI = lax.Precision.HIGHEST
NC = 5
F32 = jnp.float32
BF16 = jnp.bfloat16


def odd_rows():
    return lax.rem(lax.broadcasted_iota(jnp.int32, (8, 128), 0), 2) == 1


def spread(even, odd, mask):
    return jnp.where(mask, jnp.broadcast_to(odd, (8, 128)), jnp.broadcast_to(even, (8, 128)))


def apply(entry, columns, start=None):
    out = []
    for a in range(NC):
        total = None if start is None else start[a]
        for c in range(NC):
            term = entry(a, c)[None] * columns[c]
            total = term if total is None else total + term
        out.append(total)
    return out


def split(x):
    high = x.astype(BF16)
    return high, (x - high.astype(F32)).astype(BF16)


def kernel(n, nps, cells, flow, forcing, op, diag, lower, upper, residual, correction,
           fpad, other, force, flat, mats, maps, lead, tail, swept, corr, res, mix, work,
           summary, send_m, got_m, send_v, got_v, send_r, got_r, bounds,
           local_sem, halo_send, halo_recv, m_send, m_recv, v_send, v_recv, r_send, r_recv, out_sem):
    me, ps = lax.axis_index("row"), lax.axis_index("ps")
    per = 128 // n
    mate = 1 - ps

    loads = [
        pltpu.make_async_copy(diag, flat.at[0], local_sem.at[0]),
        pltpu.make_async_copy(lower, flat.at[1], local_sem.at[1]),
        pltpu.make_async_copy(upper, flat.at[2], local_sem.at[2]),
        pltpu.make_async_copy(flow, fpad.at[pl.ds(1, cells)], local_sem.at[3]),
        pltpu.make_async_copy(forcing, force, local_sem.at[4]),
    ]
    for load in loads:
        load.start()

    barrier = pltpu.get_barrier_semaphore()

    @pl.loop(1, n)
    def _(k):
        pl.semaphore_signal(barrier, inc=1, device_id=(lax.rem(me + k, n), ps), device_id_type=MESH)

    pl.semaphore_signal(barrier, inc=1, device_id=(me, mate), device_id_type=MESH)
    pl.semaphore_wait(barrier, n)

    to_mate = pltpu.make_async_remote_copy(
        flow, other, halo_send.at[0], halo_recv.at[0], device_id=(me, mate), device_id_type=MESH)
    up = pltpu.make_async_remote_copy(
        flow.at[cells - 1], fpad.at[0], halo_send.at[1], halo_recv.at[1],
        device_id=(lax.rem(me + 1, n), ps), device_id_type=MESH)
    down = pltpu.make_async_remote_copy(
        flow.at[0], fpad.at[cells + 1], halo_send.at[2], halo_recv.at[2],
        device_id=(lax.rem(me + n - 1, n), ps), device_id_type=MESH)
    to_mate.start()

    @pl.when(me < n - 1)
    def _():
        up.start()

    @pl.when(me > 0)
    def _():
        down.start()

    @pl.when(me == 0)
    def _():
        fpad[0] = jnp.zeros(fpad.shape[1:], F32)

    @pl.when(me == n - 1)
    def _():
        fpad[cells + 1] = jnp.zeros(fpad.shape[1:], F32)

    wide = (32, 192)
    row = lax.broadcasted_iota(jnp.int32, wide, 0)
    col = lax.broadcasted_iota(jnp.int32, wide, 1)
    part, within = col >> 5, col & 31
    left = (lax.broadcasted_iota(jnp.int32, (32, 16), 0) >> 1
            == lax.broadcasted_iota(jnp.int32, (32, 16), 1)).astype(F32)
    right = ((lax.broadcasted_iota(jnp.int32, (16, 192), 1) & 31) >> 1
             == lax.broadcasted_iota(jnp.int32, (16, 192), 0)).astype(F32)
    coupled = jnp.dot(jnp.dot(left, op[...], precision=HI, preferred_element_type=F32), right,
                      precision=HI, preferred_element_type=F32)
    swap = jnp.where((row >> 1 == within >> 1) & (row != within), F32(0.2), F32(0.0))
    coupled = jnp.where((row & 1) == (within & 1), coupled, F32(0.0))
    coef = jnp.where(part < 3, swap - coupled, jnp.where((within & 1) == ps, swap, F32(0.0)))
    rough = coef.astype(BF16).astype(F32)
    mix[...] = jnp.where((part == 2) | (part == 5), coef - rough, rough).astype(BF16)

    mask = odd_rows()
    for load in loads[:3]:
        load.wait()
    for m in range(3):
        for i in range(cells):
            mats[m, i, 0:50] = flat[m, 50 * i:50 * i + 50]
            mats[m, i, 50:56] = jnp.zeros((6, 128), F32)

    def from_diag(i):
        def entry(a, c):
            at = 10 * a + 2 * c
            return spread(mats[0, i, at:at + 1, :], mats[0, i, at + 1:at + 2, :], mask)
        return entry

    def from_maps(ref, i, base):
        def entry(a, c):
            b, at = base + (2 * c) // 8, (2 * c) % 8
            return spread(ref[i, a, b, at:at + 1, :], ref[i, a, b, at + 1:at + 2, :], mask)
        return entry

    line = lax.broadcasted_iota(jnp.int32, (2, 8, 128), 0) * 8 + lax.broadcasted_iota(jnp.int32, (2, 8, 128), 1)
    for a in range(NC):
        ident = ((line >> 1) == a).astype(F32)
        lead[0, a] = ident
        tail[cells, a, 0:2] = jnp.zeros((2, 8, 128), F32)
        tail[cells, a, 2:4] = ident

    @pl.loop(0, cells)
    def _(i):
        pairs = []
        for c in range(NC):
            low = mats[1, i, 10 * c:10 * c + 16, :].reshape(2, 8, 128)
            high = mats[2, i, 10 * c:10 * c + 16, :].reshape(2, 8, 128)
            pairs.append(jnp.concatenate([low, high], axis=0))
        made = apply(from_diag(i), pairs)
        for a in range(NC):
            maps[i, a] = -made[a]
        new = apply(from_maps(maps, i, 0), [lead[i, c] for c in range(NC)])
        for a in range(NC):
            lead[i + 1, a] = new[a]

    @pl.loop(0, cells)
    def _(k):
        i = cells - 1 - k
        start = [jnp.concatenate([lead[i + 1, a], jnp.zeros((2, 8, 128), F32)], axis=0) for a in range(NC)]
        new = apply(from_maps(maps, i, 2), [tail[i + 1, c] for c in range(NC)], start)
        for a in range(NC):
            tail[i, a] = new[a]

    def scatter_rows(value, ref):
        if per % 8 == 0:
            ref[...] = value.reshape(ref.shape)
        else:
            for j in range(n):
                ref[j, 0:per, :] = value[per * j:per * j + per, :]

    def gather_rows(ref):
        if per % 8 == 0:
            return ref[...].reshape(128, ref.shape[2])
        return jnp.concatenate([ref[j, 0:per, :] for j in range(n)], axis=0)

    def exchange(src, dst, send_sem, recv_sem):
        def copy(peer):
            return pltpu.make_async_remote_copy(
                src.at[peer], dst.at[me], send_sem.at[peer], recv_sem.at[me],
                device_id=(peer, ps), device_id_type=MESH)

        def incoming(peer):
            return pltpu.make_async_remote_copy(
                src.at[peer], dst.at[peer], send_sem.at[peer], recv_sem.at[peer],
                device_id=(peer, ps), device_id_type=MESH)

        def start():
            @pl.loop(1, n)
            def _(k):
                copy(lax.rem(me + k, n)).start()
            dst[me] = src[me]

        def wait():
            @pl.loop(1, n)
            def _(k):
                incoming(lax.rem(me + k, n)).wait_recv()

        def wait_send():
            @pl.loop(1, n)
            def _(k):
                copy(lax.rem(me + k, n)).wait_send()

        return start, wait, wait_send

    m_start, m_wait, m_sent = exchange(send_m, got_m, m_send, m_recv)
    v_start, v_wait, v_sent = exchange(send_v, got_v, v_send, v_recv)
    r_start, r_wait, r_sent = exchange(send_r, got_r, r_send, r_recv)

    for a in range(NC):
        summary[16 * a:16 * a + 16] = lead[cells, a].reshape(16, 128)
        summary[80 + 16 * a:96 + 16 * a] = tail[0, a, 0:2].reshape(16, 128)
        summary[160 + 16 * a:176 + 16 * a] = tail[0, a, 2:4].reshape(16, 128)
    summary[240:256] = jnp.zeros((16, 128), F32)
    scatter_rows(summary[0:256].T, send_m)
    m_start()

    loads[3].wait()
    loads[4].wait()
    to_mate.wait_recv()

    @pl.when(me > 0)
    def _():
        up.wait_recv()

    @pl.when(me < n - 1)
    def _():
        down.wait_recv()

    for c in range(NC):
        swept[0, c] = jnp.zeros((4, 8, 128), F32)
        corr[cells, c] = jnp.zeros((4, 8, 128), F32)

    @pl.loop(0, cells)
    def _(i):
        parts = []
        for c in range(NC):
            high, low = split(fpad[i + 1, c].reshape(32, 128))
            far_high, far_low = split(other[i, c].reshape(32, 128))
            parts.append(jnp.concatenate([high, low, high, far_high, far_low, far_high], axis=0))
        mixed = jnp.dot(mix[...], jnp.concatenate(parts, axis=1), preferred_element_type=F32)
        rows = []
        for c in range(NC):
            mine = fpad[i + 1, c]
            flatm = mine.reshape(32, 128)
            around = (fpad[i, c] + fpad[i + 2, c]
                      + (pltpu.roll(flatm, 1, 1) + pltpu.roll(flatm, 127, 1)).reshape(4, 8, 128))
            r = (force[i, c] - 1.5 * mine + 0.2 * around
                 + mixed[:, 128 * c:128 * c + 128].reshape(4, 8, 128))
            res[i, c] = r
            rows.append(r)
        scaled = apply(from_diag(i), rows)
        new = apply(from_maps(maps, i, 0), [swept[i, c] for c in range(NC)], scaled)
        for a in range(NC):
            swept[i + 1, a] = new[a]

    out_res = pltpu.make_async_copy(res, residual, out_sem.at[0])
    out_res.start()

    @pl.loop(0, cells)
    def _(k):
        i = cells - 1 - k
        new = apply(from_maps(maps, i, 2), [corr[i + 1, c] for c in range(NC)],
                    [swept[i + 1, a] for a in range(NC)])
        for a in range(NC):
            corr[i, a] = new[a]

    for a in range(NC):
        summary[32 * a:32 * a + 32] = swept[cells, a].reshape(32, 128)
        summary[160 + 32 * a:192 + 32 * a] = corr[0, a].reshape(32, 128)
    summary[320:384] = jnp.zeros((64, 128), F32)
    scatter_rows(summary[...].T, send_v)
    v_start()
    m_wait()
    bounds[0:256] = gather_rows(got_m).T
    v_wait()
    summary[...] = gather_rows(got_v).T
    lane = lax.broadcasted_iota(jnp.int32, (8, 128), 1)[None]
    steps = n.bit_length() - 1

    def shift(x, by):
        blocks = x.shape[0]
        return pltpu.roll(x.reshape(8 * blocks, 128), by, 1).reshape(blocks, 8, 128)

    for a in range(NC):
        work[0, a, 0:4] = summary[32 * a:32 * a + 32].reshape(4, 8, 128)
        work[0, a, 4:6] = bounds[16 * a:16 * a + 16].reshape(2, 8, 128)
        work[1, a, 4:6] = bounds[160 + 16 * a:176 + 16 * a].reshape(2, 8, 128)

    def scan(which, backward):
        @pl.loop(0, steps)
        def _(k):
            by = jnp.left_shift(per, k)
            turn = 128 - by if backward else by
            inside = lane < 128 - by if backward else lane >= by
            moved = [shift(work[which, c], turn) for c in range(NC)]
            old = [work[which, a] for a in range(NC)]
            start = [jnp.concatenate([old[a][0:4], jnp.zeros((2, 8, 128), F32)], axis=0) for a in range(NC)]
            new = apply(from_maps(work, which, 4), moved, start)
            for a in range(NC):
                work[which, a] = jnp.where(inside, new[a], old[a])

    scan(0, False)
    entering = [jnp.where(lane >= per, shift(work[0, a, 0:4], per), F32(0.0)) for a in range(NC)]

    def from_tail(a, c):
        at = 80 + 16 * a + 2 * c
        return spread(bounds[at:at + 1, :], bounds[at + 1:at + 2, :], mask)

    last = apply(from_tail, entering, [summary[160 + 32 * a:192 + 32 * a].reshape(4, 8, 128) for a in range(NC)])
    for a in range(NC):
        work[1, a, 0:4] = last[a]
        summary[32 * a:32 * a + 32] = entering[a].reshape(32, 128)
    scan(1, True)
    for a in range(NC):
        back = jnp.where(lane < 128 - per, shift(work[1, a, 0:4], 128 - per), F32(0.0))
        summary[160 + 32 * a:192 + 32 * a] = back.reshape(32, 128)
    scatter_rows(summary[...].T, send_r)
    r_start()
    r_wait()
    bounds[...] = gather_rows(got_r).T

    @pl.loop(0, cells)
    def _(i):
        first = [bounds[32 * c:32 * c + 32].reshape(4, 8, 128) for c in range(NC)]
        new = apply(from_maps(tail, i, 0), first, [corr[i, a] for a in range(NC)])
        second = [bounds[160 + 32 * c:192 + 32 * c].reshape(4, 8, 128) for c in range(NC)]
        new = apply(from_maps(tail, i, 2), second, new)
        for a in range(NC):
            corr[i, a] = new[a]

    out_corr = pltpu.make_async_copy(corr.at[pl.ds(0, cells)], correction, out_sem.at[1])
    out_corr.start()
    to_mate.wait_send()

    @pl.when(me < n - 1)
    def _():
        up.wait_send()

    @pl.when(me > 0)
    def _():
        down.wait_send()

    m_sent()
    v_sent()
    r_sent()
    out_res.wait()
    out_corr.wait()


def body(n, nps, flow, forcing, op, diag, lower, upper):
    cells = flow.shape[0]
    whole = flow.shape
    state = (cells, NC, 4, 8, 128)
    rows = max(8, 128 // n)
    vmem, dma = pltpu.VMEM, pltpu.SemaphoreType.DMA
    spec_any = pl.BlockSpec(memory_space=pl.ANY)
    spec_vmem = pl.BlockSpec(memory_space=pltpu.VMEM)
    residual, correction = pl.pallas_call(
        functools.partial(kernel, n, nps, cells),
        out_shape=[jax.ShapeDtypeStruct(state, F32)] * 2,
        in_specs=[spec_any, spec_any, spec_vmem, spec_any, spec_any, spec_any],
        out_specs=[spec_any, spec_any],
        scratch_shapes=[
            vmem((cells + 2,) + state[1:], F32),
            vmem(state, F32),
            vmem(state, F32),
            vmem((3, 50 * cells, 128), F32),
            vmem((3, cells, 56, 128), F32),
            vmem(state, F32),
            vmem((cells + 1, NC, 2, 8, 128), F32),
            vmem((cells + 1,) + state[1:], F32),
            vmem((cells + 1,) + state[1:], F32),
            vmem((cells + 1,) + state[1:], F32),
            vmem(state, F32),
            vmem((32, 192), BF16),
            vmem((2, NC, 6, 8, 128), F32),
            vmem((384, 128), F32),
            vmem((n, rows, 256), F32),
            vmem((n, rows, 256), F32),
            vmem((n, rows, 384), F32),
            vmem((n, rows, 384), F32),
            vmem((n, rows, 384), F32),
            vmem((n, rows, 384), F32),
            vmem((384, 128), F32),
            dma((5,)), dma((3,)), dma((3,)),
            dma((n,)), dma((n,)), dma((n,)), dma((n,)), dma((n,)), dma((n,)),
            dma((2,)),
        ],
        compiler_params=pltpu.CompilerParams(
            collective_id=0, has_side_effects=True, vmem_limit_bytes=40 * 1024 * 1024),
    )(flow.reshape(state), forcing.reshape(state), op,
      diag.reshape(50 * cells, 128), lower.reshape(50 * cells, 128), upper.reshape(50 * cells, 128))
    return residual.reshape(whole), correction.reshape(whole)


def solution(mesh):
    spec = P("row", None, None, "ps", None)
    return jax.shard_map(
        functools.partial(body, mesh.shape["row"], mesh.shape["ps"]),
        mesh=mesh,
        in_specs=(spec, spec, P(), spec, spec, spec),
        out_specs=(spec, spec),
        check_vma=False,
    )
```

profile of v0, /device:TPU:0, one launch (start us, length us, event | category | flops | bytes accessed | tf_op | source)
XLA Modules:
  0.0 39.3 jit_solution(10496354531843645187)
XLA Ops:
  0.6 0.0 copy-start.5
  0.6 0.7 %copy-done.5 = f32[16,16]{1,0:T(8,128)S(1)} copy-done((f32[16,16]{1,0:T(8,128)S(1)}, f32[16,16]{1,0:T(8,128)}, u32[]{:S(2)}) %copy-start.5) | copy-done | bytes 1048
  1.3 0.0 copy-start
  1.3 1.1 %copy-done = f32[8,5,16,2,128]{4,3,2,1,0:T(2,128)S(1)} copy-done((f32[8,5,16,2,128]{4,3,2,1,0:T(2,128)S(1)}, f32[8,5,16,2,128]{4,3,2,1,0:T(2,128)}, u32[]{:S(2)}) %copy-start) | copy-done | bytes 655384
  2.4 0.0 copy-start.1
  2.4 1.1 %copy-done.1 = f32[8,5,16,2,128]{4,3,2,1,0:T(2,128)S(1)} copy-done((f32[8,5,16,2,128]{4,3,2,1,0:T(2,128)S(1)}, f32[8,5,16,2,128]{4,3,2,1,0:T(2,128)}, u32[]{:S(2)}) %copy-start.1) | copy-done | bytes 655384
  3.5 0.0 copy-start.2
  3.5 0.9 %copy-done.2 = f32[8,5,5,2,128]{4,3,2,1,0:T(2,128)S(1)} copy-done((f32[8,5,5,2,128]{4,3,2,1,0:T(2,128)S(1)}, f32[8,5,5,2,128]{4,3,2,1,0:T(2,128)}, u32[]{:S(2)}) %copy-start.2) | copy-done | bytes 204824
  4.4 0.0 copy-start.3
  4.4 0.9 %copy-done.3 = f32[8,5,5,2,128]{4,3,2,1,0:T(2,128)S(1)} copy-done((f32[8,5,5,2,128]{4,3,2,1,0:T(2,128)S(1)}, f32[8,5,5,2,128]{4,3,2,1,0:T(2,128)}, u32[]{:S(2)}) %copy-start.3) | copy-done | bytes 204824
  5.4 0.0 copy-start.4
  5.4 0.9 %copy-done.4 = f32[8,5,5,2,128]{4,3,2,1,0:T(2,128)S(1)} copy-done((f32[8,5,5,2,128]{4,3,2,1,0:T(2,128)S(1)}, f32[8,5,5,2,128]{4,3,2,1,0:T(2,128)}, u32[]{:S(2)}) %copy-start.4) | copy-done | bytes 204824
  6.3 31.3 %shard_map.77 = (f32[8,5,4,8,128]{4,3,2,1,0:T(8,128)S(1)}, f32[8,5,4,8,128]{4,3,2,1,0:T(8,128)S(1)}) custom-call(f32[8,5,4,8,128]{4,3,2,1,0:T(8,128)S(1)} %bitcast.9, f32[8,5,4,8,128]{4,3,2,1,0:T(8,128)S(1)} %bitcast.10, f32[16,16]{1,0:T(8,128)S(1)} %copy-done.5, f32[400,128]{1,0:T(8,128)S(1)} %bitcast.11, f32[400,128]{1,0:T(8,128)S(1)} %bitcast.12, ...), custom_call_target="tpu_custom_call" | custom-call | tf_op jit(solution)/shard_map/pallas_call | solution.py:353
  37.7 0.8 %copy.10 = f32[8,5,16,2,128]{4,3,2,1,0:T(2,128)} copy(f32[8,5,16,2,128]{4,3,2,1,0:T(2,128)S(1)} %bitcast.8) | data formatting | bytes 1310720
  38.5 0.8 %copy.11 = f32[8,5,16,2,128]{4,3,2,1,0:T(2,128)} copy(f32[8,5,16,2,128]{4,3,2,1,0:T(2,128)S(1)} %bitcast.7) | data formatting | bytes 1310720
Async XLA Ops:
  0.6 0.7 %copy-start.5 = (f32[16,16]{1,0:T(8,128)S(1)}, f32[16,16]{1,0:T(8,128)}, u32[]{:S(2)}) copy-start(f32[16,16]{1,0:T(8,128)} %op.1) | copy-start | bytes 3076
  1.3 1.1 %copy-start = (f32[8,5,16,2,128]{4,3,2,1,0:T(2,128)S(1)}, f32[8,5,16,2,128]{4,3,2,1,0:T(2,128)}, u32[]{:S(2)}) copy-start(f32[8,5,16,2,128]{4,3,2,1,0:T(2,128)} %param.6) | copy-start | bytes 1966084
  2.4 1.1 %copy-start.1 = (f32[8,5,16,2,128]{4,3,2,1,0:T(2,128)S(1)}, f32[8,5,16,2,128]{4,3,2,1,0:T(2,128)}, u32[]{:S(2)}) copy-start(f32[8,5,16,2,128]{4,3,2,1,0:T(2,128)} %param.7) | copy-start | bytes 1966084
  3.5 0.9 %copy-start.2 = (f32[8,5,5,2,128]{4,3,2,1,0:T(2,128)S(1)}, f32[8,5,5,2,128]{4,3,2,1,0:T(2,128)}, u32[]{:S(2)}) copy-start(f32[8,5,5,2,128]{4,3,2,1,0:T(2,128)} %param.9) | copy-start | bytes 614404
  4.4 0.9 %copy-start.3 = (f32[8,5,5,2,128]{4,3,2,1,0:T(2,128)S(1)}, f32[8,5,5,2,128]{4,3,2,1,0:T(2,128)}, u32[]{:S(2)}) copy-start(f32[8,5,5,2,128]{4,3,2,1,0:T(2,128)} %param.10) | copy-start | bytes 614404
  5.4 0.9 %copy-start.4 = (f32[8,5,5,2,128]{4,3,2,1,0:T(2,128)S(1)}, f32[8,5,5,2,128]{4,3,2,1,0:T(2,128)}, u32[]{:S(2)}) copy-start(f32[8,5,5,2,128]{4,3,2,1,0:T(2,128)} %param.11) | copy-start | bytes 614404
where the time goes:
time: 39.7 us; the launch traced here: 39.3 us
  Pallas kernels  31.3 us (79%)
  local copies, waits for them, and re-layouts  7.33 us (18%)
  between operations  0.65 us (2%)
    pallas_call x1, Pallas kernels, body(): pl.pallas_call(functools.partial(kernel, n, nps, cells), out_shape=[jax.S...  31.3 us
    unnamed x14, local copies, waits for them, and re-layouts  7.33 us

commit v1 on v0

--- a/solution.py
+++ b/solution.py
@@ -39,7 +39,7 @@
 
 
 def kernel(n, nps, cells, flow, forcing, op, diag, lower, upper, residual, correction,
-           fpad, other, force, flat, mats, maps, lead, tail, swept, corr, res, mix, work,
+           fpad, other, below, above, force, flat, mats, maps, lead, tail, swept, corr, res, mix, work,
            summary, send_m, got_m, send_v, got_v, send_r, got_r, bounds,
            local_sem, halo_send, halo_recv, m_send, m_recv, v_send, v_recv, r_send, r_recv, out_sem):
     me, ps = lax.axis_index("row"), lax.axis_index("ps")
@@ -63,33 +63,6 @@
         pl.semaphore_signal(barrier, inc=1, device_id=(lax.rem(me + k, n), ps), device_id_type=MESH)
 
     pl.semaphore_signal(barrier, inc=1, device_id=(me, mate), device_id_type=MESH)
-    pl.semaphore_wait(barrier, n)
-
-    to_mate = pltpu.make_async_remote_copy(
-        flow, other, halo_send.at[0], halo_recv.at[0], device_id=(me, mate), device_id_type=MESH)
-    up = pltpu.make_async_remote_copy(
-        flow.at[cells - 1], fpad.at[0], halo_send.at[1], halo_recv.at[1],
-        device_id=(lax.rem(me + 1, n), ps), device_id_type=MESH)
-    down = pltpu.make_async_remote_copy(
-        flow.at[0], fpad.at[cells + 1], halo_send.at[2], halo_recv.at[2],
-        device_id=(lax.rem(me + n - 1, n), ps), device_id_type=MESH)
-    to_mate.start()
-
-    @pl.when(me < n - 1)
-    def _():
-        up.start()
-
-    @pl.when(me > 0)
-    def _():
-        down.start()
-
-    @pl.when(me == 0)
-    def _():
-        fpad[0] = jnp.zeros(fpad.shape[1:], F32)
-
-    @pl.when(me == n - 1)
-    def _():
-        fpad[cells + 1] = jnp.zeros(fpad.shape[1:], F32)
 
     wide = (32, 192)
     row = lax.broadcasted_iota(jnp.int32, wide, 0)
@@ -105,7 +78,9 @@
     coupled = jnp.where((row & 1) == (within & 1), coupled, F32(0.0))
     coef = jnp.where(part < 3, swap - coupled, jnp.where((within & 1) == ps, swap, F32(0.0)))
     rough = coef.astype(BF16).astype(F32)
-    mix[...] = jnp.where((part == 2) | (part == 5), coef - rough, rough).astype(BF16)
+    pieces = jnp.where((part == 2) | (part == 5), coef - rough, rough).astype(BF16)
+    mix[0] = pieces[:, 0:96]
+    mix[1] = pieces[:, 96:192]
 
     mask = odd_rows()
     for load in loads[:3]:
@@ -207,40 +182,71 @@
         summary[160 + 16 * a:176 + 16 * a] = tail[0, a, 2:4].reshape(16, 128)
     summary[240:256] = jnp.zeros((16, 128), F32)
     scatter_rows(summary[0:256].T, send_m)
-    m_start()
-
     loads[3].wait()
     loads[4].wait()
-    to_mate.wait_recv()
-
-    @pl.when(me > 0)
-    def _():
-        up.wait_recv()
-
-    @pl.when(me < n - 1)
-    def _():
-        down.wait_recv()
-
-    for c in range(NC):
-        swept[0, c] = jnp.zeros((4, 8, 128), F32)
-        corr[cells, c] = jnp.zeros((4, 8, 128), F32)
-
-    @pl.loop(0, cells)
-    def _(i):
+    fpad[0] = jnp.zeros(fpad.shape[1:], F32)
+    fpad[cells + 1] = jnp.zeros(fpad.shape[1:], F32)
+
+    def mixed(ref, i, first):
         parts = []
         for c in range(NC):
-            high, low = split(fpad[i + 1, c].reshape(32, 128))
-            far_high, far_low = split(other[i, c].reshape(32, 128))
-            parts.append(jnp.concatenate([high, low, high, far_high, far_low, far_high], axis=0))
-        mixed = jnp.dot(mix[...], jnp.concatenate(parts, axis=1), preferred_element_type=F32)
-        rows = []
+            high, low = split(ref[i, c].reshape(32, 128))
+            parts.append(jnp.concatenate([high, low, high], axis=0))
+        return jnp.dot(mix[first], jnp.concatenate(parts, axis=1), preferred_element_type=F32)
+
+    @pl.loop(0, cells)
+    def _(i):
+        sums = mixed(fpad, i + 1, 0)
         for c in range(NC):
             mine = fpad[i + 1, c]
             flatm = mine.reshape(32, 128)
             around = (fpad[i, c] + fpad[i + 2, c]
                       + (pltpu.roll(flatm, 1, 1) + pltpu.roll(flatm, 127, 1)).reshape(4, 8, 128))
-            r = (force[i, c] - 1.5 * mine + 0.2 * around
-                 + mixed[:, 128 * c:128 * c + 128].reshape(4, 8, 128))
+            res[i, c] = (force[i, c] - 1.5 * mine + 0.2 * around
+                         + sums[:, 128 * c:128 * c + 128].reshape(4, 8, 128))
+
+    pl.semaphore_wait(barrier, n)
+    to_mate = pltpu.make_async_remote_copy(
+        fpad.at[pl.ds(1, cells)], other, halo_send.at[0], halo_recv.at[0], device_id=(me, mate), device_id_type=MESH)
+    up = pltpu.make_async_remote_copy(
+        fpad.at[cells], below, halo_send.at[1], halo_recv.at[1],
+        device_id=(lax.rem(me + 1, n), ps), device_id_type=MESH)
+    down = pltpu.make_async_remote_copy(
+        fpad.at[1], above, halo_send.at[2], halo_recv.at[2],
+        device_id=(lax.rem(me + n - 1, n), ps), device_id_type=MESH)
+    to_mate.start()
+
+    @pl.when(me < n - 1)
+    def _():
+        up.start()
+
+    @pl.when(me > 0)
+    def _():
+        down.start()
+
+    m_start()
+    to_mate.wait_recv()
+
+    @pl.when(me > 0)
+    def _():
+        up.wait_recv()
+        res[0] += 0.2 * below[...]
+
+    @pl.when(me < n - 1)
+    def _():
+        down.wait_recv()
+        res[cells - 1] += 0.2 * above[...]
+
+    for c in range(NC):
+        swept[0, c] = jnp.zeros((4, 8, 128), F32)
+        corr[cells, c] = jnp.zeros((4, 8, 128), F32)
+
+    @pl.loop(0, cells)
+    def _(i):
+        sums = mixed(other, i, 1)
+        rows = []
+        for c in range(NC):
+            r = res[i, c] + sums[:, 128 * c:128 * c + 128].reshape(4, 8, 128)
             res[i, c] = r
             rows.append(r)
         scaled = apply(from_diag(i), rows)
@@ -348,7 +354,7 @@
     state = (cells, NC, 4, 8, 128)
     rows = max(8, 128 // n)
     vmem, dma = pltpu.VMEM, pltpu.SemaphoreType.DMA
-    spec_any = pl.BlockSpec(memory_space=pl.ANY)
+    spec_any = pl.BlockSpec(memory_space=pltpu.HBM)
     spec_vmem = pl.BlockSpec(memory_space=pltpu.VMEM)
     residual, correction = pl.pallas_call(
         functools.partial(kernel, n, nps, cells),
@@ -358,6 +364,8 @@
         scratch_shapes=[
             vmem((cells + 2,) + state[1:], F32),
             vmem(state, F32),
+            vmem(state[1:], F32),
+            vmem(state[1:], F32),
             vmem(state, F32),
             vmem((3, 50 * cells, 128), F32),
             vmem((3, cells, 56, 128), F32),
@@ -367,7 +375,7 @@
             vmem((cells + 1,) + state[1:], F32),
             vmem((cells + 1,) + state[1:], F32),
             vmem(state, F32),
-            vmem((32, 192), BF16),
+            vmem((2, 32, 96), BF16),
             vmem((2, NC, 6, 8, 128), F32),
             vmem((384, 128), F32),
             vmem((n, rows, 256), F32),
@@ -382,7 +390,7 @@
             dma((2,)),
         ],
         compiler_params=pltpu.CompilerParams(
-            collective_id=0, has_side_effects=True, vmem_limit_bytes=40 * 1024 * 1024),
+            collective_id=0, has_side_effects=True, vmem_limit_bytes=60 * 1024 * 1024),
     )(flow.reshape(state), forcing.reshape(state), op,
       diag.reshape(50 * cells, 128), lower.reshape(50 * cells, 128), upper.reshape(50 * cells, 128))
     return residual.reshape(whole), correction.reshape(whole)

time: 39.7 us -> 34.3 us (0.86)
  local copies, waits for them, and re-layouts: 7.33 us -> 2.88 us
  Pallas kernels: 31.3 us -> 30.5 us
    unnamed x14 -> x4, local copies, waits for them, and re-layouts: 7.33 us -> 2.88 us
    pallas_call x1, Pallas kernels: 31.3 us -> 30.5 us  [body(): pl.pallas_call(functools.partial(kernel, n, nps, cells), out_shape=[jax.S...]
where the time goes in v1:
time: 34.3 us; the launch traced here: 34.1 us
  Pallas kernels  30.5 us (89%)
  local copies, waits for them, and re-layouts  2.88 us (8%)
  between operations  0.65 us (2%)
    pallas_call x1, Pallas kernels, body(): pl.pallas_call(functools.partial(kernel, n, nps, cells), out_shape=[jax.S...  30.5 us
    unnamed x4, local copies, waits for them, and re-layouts  2.88 us

profile of v1, /device:TPU:0, one launch (start us, length us, event | category | flops | bytes accessed | tf_op | source)
XLA Modules:
  0.0 34.1 jit_solution(6652590891501018528)
XLA Ops:
  0.6 30.5 %shard_map.77 = (f32[8,5,4,8,128]{4,3,2,1,0:T(8,128)}, f32[8,5,4,8,128]{4,3,2,1,0:T(8,128)}) custom-call(f32[8,5,4,8,128]{4,3,2,1,0:T(8,128)} %bitcast.9, f32[8,5,4,8,128]{4,3,2,1,0:T(8,128)} %bitcast.10, f32[16,16]{1,0:T(8,128)} %op.1, f32[400,128]{1,0:T(8,128)} %bitcast.11, f32[400,128]{1,0:T(8,128)} %bitcast.12, f32[400,128]{1,0:T(8,128)} %bitcast.13), custom_call_target="tpu_custom_call" | custom-call | tf_op jit(solution)/shard_map/pallas_call | solution.py:359
  31.2 0.0 copy-start
  31.2 2.0 %copy.10 = f32[8,5,16,2,128]{4,3,2,1,0:T(2,128)} copy(f32[8,5,16,2,128]{4,3,2,1,0:T(2,128)} %bitcast.8) | data formatting | bytes 1310720
  33.2 0.0 copy-done
  33.2 0.8 %copy.11 = f32[8,5,16,2,128]{4,3,2,1,0:T(2,128)} copy(f32[8,5,16,2,128]{4,3,2,1,0:T(2,128)S(1)} %bitcast.7) | data formatting | bytes 1310720
Async XLA Ops:
  31.2 2.0 %copy-start = (f32[8,5,4,8,128]{4,3,2,1,0:T(8,128)S(1)}, f32[8,5,4,8,128]{4,3,2,1,0:T(8,128)}, u32[]{:S(2)}) copy-start(f32[8,5,4,8,128]{4,3,2,1,0:T(8,128)} %get-tuple-element.5) | copy-start | bytes 1966084

commit v2 on v1

--- a/solution.py
+++ b/solution.py
@@ -38,10 +38,10 @@
     return high, (x - high.astype(F32)).astype(BF16)
 
 
-def kernel(n, nps, cells, flow, forcing, op, diag, lower, upper, residual, correction,
-           fpad, other, below, above, force, flat, mats, maps, lead, tail, swept, corr, res, mix, work,
+def kernel(n, nps, cells, flow, forcing, op, diag, lower, upper, res, correction,
+           harmonics, fpad, other, below, above, force, flat, mats, maps, lead, tail, swept, corr, mix, work,
            summary, send_m, got_m, send_v, got_v, send_r, got_r, bounds,
-           local_sem, halo_send, halo_recv, m_send, m_recv, v_send, v_recv, r_send, r_recv, out_sem):
+           local_sem, halo_send, halo_recv, m_send, m_recv, v_send, v_recv, r_send, r_recv):
     me, ps = lax.axis_index("row"), lax.axis_index("ps")
     per = 128 // n
     mate = 1 - ps
@@ -52,6 +52,7 @@
         pltpu.make_async_copy(upper, flat.at[2], local_sem.at[2]),
         pltpu.make_async_copy(flow, fpad.at[pl.ds(1, cells)], local_sem.at[3]),
         pltpu.make_async_copy(forcing, force, local_sem.at[4]),
+        pltpu.make_async_copy(op, harmonics, local_sem.at[5]),
     ]
     for load in loads:
         load.start()
@@ -63,6 +64,25 @@
         pl.semaphore_signal(barrier, inc=1, device_id=(lax.rem(me + k, n), ps), device_id_type=MESH)
 
     pl.semaphore_signal(barrier, inc=1, device_id=(me, mate), device_id_type=MESH)
+
+    pl.semaphore_wait(barrier, n)
+    to_mate = pltpu.make_async_remote_copy(
+        flow, other, halo_send.at[0], halo_recv.at[0], device_id=(me, mate), device_id_type=MESH)
+    up = pltpu.make_async_remote_copy(
+        flow.at[cells - 1], below, halo_send.at[1], halo_recv.at[1],
+        device_id=(lax.rem(me + 1, n), ps), device_id_type=MESH)
+    down = pltpu.make_async_remote_copy(
+        flow.at[0], above, halo_send.at[2], halo_recv.at[2],
+        device_id=(lax.rem(me + n - 1, n), ps), device_id_type=MESH)
+    to_mate.start()
+
+    @pl.when(me < n - 1)
+    def _():
+        up.start()
+
+    @pl.when(me > 0)
+    def _():
+        down.start()
 
     wide = (32, 192)
     row = lax.broadcasted_iota(jnp.int32, wide, 0)
@@ -72,7 +92,8 @@
             == lax.broadcasted_iota(jnp.int32, (32, 16), 1)).astype(F32)
     right = ((lax.broadcasted_iota(jnp.int32, (16, 192), 1) & 31) >> 1
              == lax.broadcasted_iota(jnp.int32, (16, 192), 0)).astype(F32)
-    coupled = jnp.dot(jnp.dot(left, op[...], precision=HI, preferred_element_type=F32), right,
+    loads[5].wait()
+    coupled = jnp.dot(jnp.dot(left, harmonics[...], precision=HI, preferred_element_type=F32), right,
                       precision=HI, preferred_element_type=F32)
     swap = jnp.where((row >> 1 == within >> 1) & (row != within), F32(0.2), F32(0.0))
     coupled = jnp.where((row & 1) == (within & 1), coupled, F32(0.0))
@@ -144,37 +165,22 @@
         return jnp.concatenate([ref[j, 0:per, :] for j in range(n)], axis=0)
 
     def exchange(src, dst, send_sem, recv_sem):
-        def copy(peer):
-            return pltpu.make_async_remote_copy(
-                src.at[peer], dst.at[me], send_sem.at[peer], recv_sem.at[me],
-                device_id=(peer, ps), device_id_type=MESH)
-
-        def incoming(peer):
-            return pltpu.make_async_remote_copy(
-                src.at[peer], dst.at[peer], send_sem.at[peer], recv_sem.at[peer],
-                device_id=(peer, ps), device_id_type=MESH)
-
         def start():
-            @pl.loop(1, n)
-            def _(k):
-                copy(lax.rem(me + k, n)).start()
+            for k in range(1, n):
+                peer = lax.rem(me + k, n)
+                pltpu.make_async_remote_copy(
+                    src.at[peer], dst.at[me], send_sem, recv_sem,
+                    device_id=(peer, ps), device_id_type=MESH).start()
             dst[me] = src[me]
 
-        def wait():
-            @pl.loop(1, n)
-            def _(k):
-                incoming(lax.rem(me + k, n)).wait_recv()
-
-        def wait_send():
-            @pl.loop(1, n)
-            def _(k):
-                copy(lax.rem(me + k, n)).wait_send()
-
-        return start, wait, wait_send
-
-    m_start, m_wait, m_sent = exchange(send_m, got_m, m_send, m_recv)
-    v_start, v_wait, v_sent = exchange(send_v, got_v, v_send, v_recv)
-    r_start, r_wait, r_sent = exchange(send_r, got_r, r_send, r_recv)
+        every = pltpu.make_async_remote_copy(
+            src.at[pl.ds(0, n - 1)], dst.at[pl.ds(0, n - 1)], send_sem, recv_sem,
+            device_id=(lax.rem(me + 1, n), ps), device_id_type=MESH)
+        return start, every.wait_recv, every.wait_send
+
+    m_start, m_wait, m_sent = exchange(send_m, got_m, m_send.at[0], m_recv.at[0])
+    v_start, v_wait, v_sent = exchange(send_v, got_v, v_send.at[0], v_recv.at[0])
+    r_start, r_wait, r_sent = exchange(send_r, got_r, r_send.at[0], r_recv.at[0])
 
     for a in range(NC):
         summary[16 * a:16 * a + 16] = lead[cells, a].reshape(16, 128)
@@ -182,6 +188,7 @@
         summary[160 + 16 * a:176 + 16 * a] = tail[0, a, 2:4].reshape(16, 128)
     summary[240:256] = jnp.zeros((16, 128), F32)
     scatter_rows(summary[0:256].T, send_m)
+    m_start()
     loads[3].wait()
     loads[4].wait()
     fpad[0] = jnp.zeros(fpad.shape[1:], F32)
@@ -205,26 +212,6 @@
             res[i, c] = (force[i, c] - 1.5 * mine + 0.2 * around
                          + sums[:, 128 * c:128 * c + 128].reshape(4, 8, 128))
 
-    pl.semaphore_wait(barrier, n)
-    to_mate = pltpu.make_async_remote_copy(
-        fpad.at[pl.ds(1, cells)], other, halo_send.at[0], halo_recv.at[0], device_id=(me, mate), device_id_type=MESH)
-    up = pltpu.make_async_remote_copy(
-        fpad.at[cells], below, halo_send.at[1], halo_recv.at[1],
-        device_id=(lax.rem(me + 1, n), ps), device_id_type=MESH)
-    down = pltpu.make_async_remote_copy(
-        fpad.at[1], above, halo_send.at[2], halo_recv.at[2],
-        device_id=(lax.rem(me + n - 1, n), ps), device_id_type=MESH)
-    to_mate.start()
-
-    @pl.when(me < n - 1)
-    def _():
-        up.start()
-
-    @pl.when(me > 0)
-    def _():
-        down.start()
-
-    m_start()
     to_mate.wait_recv()
 
     @pl.when(me > 0)
@@ -253,9 +240,6 @@
         new = apply(from_maps(maps, i, 0), [swept[i, c] for c in range(NC)], scaled)
         for a in range(NC):
             swept[i + 1, a] = new[a]
-
-    out_res = pltpu.make_async_copy(res, residual, out_sem.at[0])
-    out_res.start()
 
     @pl.loop(0, cells)
     def _(k):
@@ -327,10 +311,8 @@
         second = [bounds[160 + 32 * c:192 + 32 * c].reshape(4, 8, 128) for c in range(NC)]
         new = apply(from_maps(tail, i, 2), second, new)
         for a in range(NC):
-            corr[i, a] = new[a]
-
-    out_corr = pltpu.make_async_copy(corr.at[pl.ds(0, cells)], correction, out_sem.at[1])
-    out_corr.start()
+            correction[i, a] = new[a]
+
     to_mate.wait_send()
 
     @pl.when(me < n - 1)
@@ -344,8 +326,20 @@
     m_sent()
     v_sent()
     r_sent()
-    out_res.wait()
-    out_corr.wait()
+
+
+def deliver(residual, correction, out_residual, out_correction, sems):
+    copies = [pltpu.make_async_copy(src.at[i], dst.at[i], sems.at[k, i])
+              for k, (src, dst) in enumerate(((residual, out_residual), (correction, out_correction)))
+              for i in range(src.shape[0])]
+    for copy in copies:
+        copy.start()
+    for copy in copies:
+        copy.wait()
+
+
+def pin(x):
+    return pltpu.with_memory_space_constraint(x, pltpu.HBM)
 
 
 def body(n, nps, flow, forcing, op, diag, lower, upper):
@@ -359,9 +353,10 @@
     residual, correction = pl.pallas_call(
         functools.partial(kernel, n, nps, cells),
         out_shape=[jax.ShapeDtypeStruct(state, F32)] * 2,
-        in_specs=[spec_any, spec_any, spec_vmem, spec_any, spec_any, spec_any],
-        out_specs=[spec_any, spec_any],
+        in_specs=[spec_any] * 6,
+        out_specs=[spec_vmem, spec_vmem],
         scratch_shapes=[
+            vmem((16, 16), F32),
             vmem((cells + 2,) + state[1:], F32),
             vmem(state, F32),
             vmem(state[1:], F32),
@@ -374,7 +369,6 @@
             vmem((cells + 1,) + state[1:], F32),
             vmem((cells + 1,) + state[1:], F32),
             vmem((cells + 1,) + state[1:], F32),
-            vmem(state, F32),
             vmem((2, 32, 96), BF16),
             vmem((2, NC, 6, 8, 128), F32),
             vmem((384, 128), F32),
@@ -385,14 +379,21 @@
             vmem((n, rows, 384), F32),
             vmem((n, rows, 384), F32),
             vmem((384, 128), F32),
-            dma((5,)), dma((3,)), dma((3,)),
-            dma((n,)), dma((n,)), dma((n,)), dma((n,)), dma((n,)), dma((n,)),
-            dma((2,)),
+            dma((6,)), dma((3,)), dma((3,)),
+            dma((1,)), dma((1,)), dma((1,)), dma((1,)), dma((1,)), dma((1,)),
         ],
         compiler_params=pltpu.CompilerParams(
-            collective_id=0, has_side_effects=True, vmem_limit_bytes=60 * 1024 * 1024),
-    )(flow.reshape(state), forcing.reshape(state), op,
-      diag.reshape(50 * cells, 128), lower.reshape(50 * cells, 128), upper.reshape(50 * cells, 128))
+            collective_id=0, has_side_effects=True, vmem_limit_bytes=40 * 1024 * 1024),
+    )(pin(flow.reshape(state)), pin(forcing.reshape(state)), pin(op),
+      pin(diag.reshape(50 * cells, 128)), pin(lower.reshape(50 * cells, 128)), pin(upper.reshape(50 * cells, 128)))
+    residual, correction = pl.pallas_call(
+        deliver,
+        out_shape=[jax.ShapeDtypeStruct(state, F32)] * 2,
+        in_specs=[pl.BlockSpec(memory_space=pltpu.VMEM)] * 2,
+        out_specs=[spec_any] * 2,
+        scratch_shapes=[dma((2, cells))],
+        compiler_params=pltpu.CompilerParams(vmem_limit_bytes=8 * 1024 * 1024),
+    )(residual, correction)
     return residual.reshape(whole), correction.reshape(whole)
 
 

time: 34.3 us -> 30.4 us (0.89)
  local copies, waits for them, and re-layouts: 2.88 us -> 0 us
  Pallas kernels: 30.5 us -> 29.6 us
    unnamed x4 -> x0, local copies, waits for them, and re-layouts: 2.88 us -> none
    pallas_call x1, Pallas kernels: 30.5 us -> 28.4 us  [body(): pl.pallas_call(functools.partial(kernel, n, nps, cells), out_shape=[jax.S...]
    pallas_call x0 -> x1, Pallas kernels: none -> 1.18 us  [body(): pl.pallas_call(deliver, out_shape=[jax.ShapeDtypeStruct(state, F32)] * 2,...]
where the time goes in v2:
time: 30.4 us; the launch traced here: 30.3 us
  Pallas kernels  29.6 us (97%)
  between operations  0.64 us (2%)
    pallas_call x1, Pallas kernels, body(): pl.pallas_call(functools.partial(kernel, n, nps, cells), out_shape=[jax.S...  28.4 us
    pallas_call x1, Pallas kernels, body(): pl.pallas_call(deliver, out_shape=[jax.ShapeDtypeStruct(state, F32)] * 2,...  1.18 us

profile of v2, /device:TPU:0, one launch (start us, length us, event | category | flops | bytes accessed | tf_op | source)
XLA Modules:
  0.0 30.3 jit_solution(16550880674585374312)
XLA Ops:
  0.6 28.4 %shard_map.77 = (f32[8,5,4,8,128]{4,3,2,1,0:T(8,128)S(1)}, f32[8,5,4,8,128]{4,3,2,1,0:T(8,128)S(1)}) custom-call(f32[8,5,4,8,128]{4,3,2,1,0:T(8,128)} %bitcast.7, f32[8,5,4,8,128]{4,3,2,1,0:T(8,128)} %bitcast.8, f32[16,16]{1,0:T(8,128)} %op.1, f32[400,128]{1,0:T(8,128)} %bitcast.9, f32[400,128]{1,0:T(8,128)} %bitcast.10, f32[400,128]{1,0:T(8,128)} %bitcast.11), custom_call_target="tpu_custom_call" | custom-call | tf_op jit(solution)/shard_map/pallas_call | solution.py:353
  29.1 1.2 %shard_map.78 = (f32[8,5,4,8,128]{4,3,2,1,0:T(8,128)}, f32[8,5,4,8,128]{4,3,2,1,0:T(8,128)}) custom-call(f32[8,5,4,8,128]{4,3,2,1,0:T(8,128)S(1)} %get-tuple-element.6.residual, f32[8,5,4,8,128]{4,3,2,1,0:T(8,128)S(1)} %get-tuple-element.7.correction), custom_call_target="tpu_custom_call" | custom-call | tf_op jit(solution)/shard_map/pallas_call | solution.py:389
